TPU v7x, 32 devices: a whole 2x2x4 slice. The times are simulated.
32 devices in a mesh: ctx: 16 (over z, y, x), tp: 2 (over core).
Axes of the slice: x: 2, y: 2, z: 4, core: 2. Of those that a mesh axis runs over, the one named last changes fastest.
Arguments:
- queries: bfloat16 [12288, 8192], P('ctx', 'tp'), may hold values from -6 to 6
- keys: bfloat16 [12288, 8192], P('ctx', 'tp'), may hold values from -6 to 6
- values: bfloat16 [12288, 8192], P('ctx', 'tp'), may hold values from -40 to 40
- out_grad: bfloat16 [12288, 8192], P('ctx', 'tp'), may hold values from -6 to 6
- gain: float32 [8192], P('tp'), may hold values from 0.1 to 1.9
- doc_ids: int32 [12288], P('ctx'), may hold values from 0 to 3, never falling along the last dimension, each value on 1 to 6144 neighbouring positions
Outputs:
- normed: bfloat16 [12288, 8192], P('ctx', 'tp')
- grad_query: bfloat16 [12288, 8192], P('ctx', 'tp')
- grad_key: bfloat16 [12288, 8192], P('ctx', 'tp')
- grad_value: bfloat16 [12288, 8192], P('ctx', 'tp')
Inputs may be any that keep to these rules, and one draw needn't show every extreme that they name: doc_ids never fall along the sequence; every one of the 4 documents has 1 to 6144 tokens and one has exactly 6144.
All inputs are finite; a program needn't handle non-finite values.
Results may differ from a plain program's by a relative error of at most 0.0062.
Values may be sent and summed in bfloat16 or wider, within the bound.
A program may use at most 256 MiB of HBM per device.

v0:
```python
import jax
import jax.numpy as jnp
from jax import lax
from jax.sharding import PartitionSpec as P

HEADS = 64
HD = 128


NORM_EPS = 1e-06


def shards(queries, keys, values, out_grad, gain, doc_ids):
    tokens_here = queries.shape[0]
    heads_here = queries.shape[1] // HD
    width_all = HEADS * HD
    flat_width = heads_here * HD
    query_heads = queries.reshape(tokens_here, heads_here, HD).transpose(1, 0, 2)
    key_heads = keys.reshape(tokens_here, heads_here, HD).transpose(1, 0, 2)
    value_heads = values.reshape(tokens_here, heads_here, HD).transpose(1, 0, 2)
    position = jnp.arange(tokens_here)
    doc_mask = (
        (doc_ids[:, None] == doc_ids[None, :]) & (position[:, None] >= position[None, :])
    ).astype(jnp.bfloat16)
    first_doc = doc_ids[0]
    last_doc = doc_ids[tokens_here - 1]
    first_rows = (doc_ids == first_doc).astype(jnp.bfloat16)[None, :, None]
    last_rows = (doc_ids == last_doc).astype(jnp.bfloat16)[None, :, None]
    query_first = query_heads * first_rows
    key_last = key_heads * last_rows
    value_last = value_heads * last_rows
    own_state = jnp.einsum(
        "hta,htb->hab", key_last, value_heads, preferred_element_type=jnp.float32
    ).astype(jnp.bfloat16)
    device_rank = lax.axis_index("ctx")
    blocks = lax.all_gather(own_state.reshape(1, heads_here * HD, HD), "ctx", axis=0, tiled=True)
    doc_tags = lax.all_gather(last_doc.astype(jnp.bfloat16).reshape(1), "ctx", axis=0, tiled=True)
    ranks_seen = jnp.arange(blocks.shape[0])
    weights = ((ranks_seen < device_rank) & (doc_tags == first_doc.astype(jnp.bfloat16))).astype(
        jnp.bfloat16
    )
    summed = jnp.einsum("n,nab->ab", weights, blocks, preferred_element_type=jnp.float32)
    incoming = summed.reshape(heads_here, HD, HD).astype(jnp.bfloat16)
    scores = (
        jnp.einsum("hta,hsa->hts", query_heads, key_heads, preferred_element_type=jnp.float32)
        * doc_mask[None]
    ).astype(jnp.bfloat16)
    attended_heads = jnp.einsum(
        "htk,hkb->htb",
        jnp.concatenate([scores, query_first], axis=2),
        jnp.concatenate([value_heads, incoming], axis=1),
        preferred_element_type=jnp.float32,
    )
    flat = attended_heads.transpose(1, 0, 2).reshape(tokens_here, flat_width)
    scaled_grad = gain[None, :] * out_grad.astype(jnp.float32)
    square_sum, cross_sum = lax.psum(
        (jnp.sum(flat * flat, axis=1), jnp.sum(scaled_grad * flat, axis=1)), "tp"
    )
    inverse = lax.rsqrt(square_sum / width_all + NORM_EPS)
    normed = (flat * inverse[:, None] * gain[None, :]).astype(jnp.bfloat16)
    delta = (
        inverse[:, None] * scaled_grad - flat * (inverse**3 * cross_sum / width_all)[:, None]
    ).astype(jnp.bfloat16)
    delta_heads = delta.reshape(tokens_here, heads_here, HD).transpose(1, 0, 2)
    own_reverse = jnp.einsum(
        "hta,htb->hab", query_first, delta_heads, preferred_element_type=jnp.float32
    ).astype(jnp.bfloat16)
    device_place = lax.axis_index("ctx")
    blocks = lax.all_gather(own_reverse.reshape(1, heads_here * HD, HD), "ctx", axis=0, tiled=True)
    doc_tags = lax.all_gather(first_doc.astype(jnp.bfloat16).reshape(1), "ctx", axis=0, tiled=True)
    ranks_seen = jnp.arange(blocks.shape[0])
    weights = ((ranks_seen > device_place) & (doc_tags == last_doc.astype(jnp.bfloat16))).astype(
        jnp.bfloat16
    )
    gathered = jnp.einsum("n,nab->ab", weights, blocks, preferred_element_type=jnp.float32)
    outgoing = gathered.reshape(heads_here, HD, HD).astype(jnp.bfloat16)
    dscores = (
        jnp.einsum("htb,hsb->hts", delta_heads, value_heads, preferred_element_type=jnp.float32)
        * doc_mask[None]
    ).astype(jnp.bfloat16)
    grad_query = jnp.einsum(
        "htk,hka->hta",
        jnp.concatenate([dscores, delta_heads * first_rows], axis=2),
        jnp.concatenate([key_heads, incoming.transpose(0, 2, 1)], axis=1),
        preferred_element_type=jnp.float32,
    )
    grad_key = jnp.einsum(
        "hks,hka->hsa",
        jnp.concatenate([dscores, value_last.transpose(0, 2, 1)], axis=1),
        jnp.concatenate([query_heads, outgoing.transpose(0, 2, 1)], axis=1),
        preferred_element_type=jnp.float32,
    )
    grad_value = jnp.einsum(
        "hks,hkb->hsb",
        jnp.concatenate([scores, key_last.transpose(0, 2, 1)], axis=1),
        jnp.concatenate([delta_heads, outgoing], axis=1),
        preferred_element_type=jnp.float32,
    )
    return (
        normed,
        grad_query.astype(jnp.bfloat16).transpose(1, 0, 2).reshape(tokens_here, flat_width),
        grad_key.astype(jnp.bfloat16).transpose(1, 0, 2).reshape(tokens_here, flat_width),
        grad_value.astype(jnp.bfloat16).transpose(1, 0, 2).reshape(tokens_here, flat_width),
    )


def solution(mesh):
    in_specs = (P("ctx", "tp"), P("ctx", "tp"), P("ctx", "tp"), P("ctx", "tp"), P("tp"), P("ctx"))
    out_specs = (P("ctx", "tp"), P("ctx", "tp"), P("ctx", "tp"), P("ctx", "tp"))
    return jax.shard_map(shards, mesh=mesh, in_specs=in_specs, out_specs=out_specs, check_vma=False)
```

profile of v0, /device:TPU:0, one launch (start us, length us, event | category | flops | bytes accessed | tf_op | source)
XLA Modules:
  0.0 586.8 jit_solution(9548414641189832393)
XLA Ops:
  7.2 0.0 all-gather.3.cloned.1.call-start
  7.2 1.3 fusion.85
  8.6 8.6 %copy.46 = bf16[768,4096]{0,1:T(8,128)(2,1)} copy(bf16[768,4096]{1,0:T(8,128)(2,1)} %param.7) | data formatting | bytes 12582912 | tf_op args[1]
  17.2 0.0 copy-start.1
  17.2 8.6 %copy.48 = bf16[768,4096]{0,1:T(8,128)(2,1)} copy(bf16[768,4096]{1,0:T(8,128)(2,1)} %param.8) | data formatting | bytes 12582912 | tf_op args[2]
  25.8 0.0 copy-done.1
  25.8 1.3 compare_convert_fusion
  27.1 0.0 copy-start.3
  27.1 7.4 %fusion.58 = bf16[32,128,128]{2,1,0:T(8,128)(2,1)} fusion(bf16[32,768,128]{1,2,0:T(8,128)(2,1)} %bitcast.82, bf16[32,768,128]{1,2,0:T(8,128)(2,1)} %bitcast.78, bf16[768]{0:T(1024)(128)(2,1)S(1)} %get-tuple-element.24), kind=kOutput, calls=%fused_computation.58 | convolution fusion | flops 808976384 | bytes 13633024 | tf_op jit(solution)/shard_map/hta,htb->hab/dot_general | solution.py:32
  34.5 0.0 all-gather.3.cloned.1.call-update
  34.5 0.0 all-gather.5.cloned.1.call-start
  35.9 0.0 copy-done.3
  35.9 0.6 dynamic-slice
  36.5 0.8 dynamic-update-slice
  37.3 0.8 dynamic-update-slice.1
  38.0 45.2 %all-reduce.3 = (bf16[16]{0:T(256)(128)(2,1)S(1)}, bf16[16]{0:T(256)(128)(2,1)}) all-reduce(bf16[16]{0:T(256)(128)(2,1)S(1)} %dynamic-update-slice, bf16[16]{0:T(256)(128)(2,1)S(1)} %dynamic-update-slice.1), channel_id=1, replica_groups=mesh['ctx'=16,'tp'=2] {'ctx'}, use_global_device_ids=true, to_apply=%add | all-reduce | flops 32 | bytes 128
  83.2 8.6 %copy.44 = bf16[768,4096]{0,1:T(8,128)(2,1)} copy(bf16[768,4096]{1,0:T(8,128)(2,1)} %param.6) | data formatting | bytes 12582912 | tf_op args[0]
  91.8 8.5 %copy.45 = bf16[768,32,128]{2,0,1:T(8,128)(2,1)} copy(bf16[768,32,128]{0,2,1:T(8,128)(2,1)} %bitcast.87) | data formatting | bytes 12582912 | tf_op jit(solution)/shard_map/reshape | solution.py:18
  100.4 8.6 %copy.51 = bf16[768,4096]{0,1:T(8,128)(2,1)} copy(bf16[768,4096]{1,0:T(8,128)(2,1)} %param.9) | data formatting | bytes 12582912 | tf_op args[3]
  109.0 0.3 fusion.61
  109.2 6.0 %broadcast_multiply_fusion.1 = bf16[32,768,128]{2,1,0:T(8,128)(2,1)} fusion(bf16[768]{0:T(1024)(128)(2,1)S(1)} %get-tuple-element.25, bf16[768,32,128]{2,0,1:T(8,128)(2,1)} %copy.45), kind=kLoop, calls=%fused_computation.54 | loop fusion | flops 3145728 | bytes 12584448 | tf_op jit(solution)/shard_map/mul | solution.py:29
  115.2 20.4 %multiply_convert_fusion.1 = bf16[32,768,768]{2,1,0:T(8,128)(2,1)} fusion(f32[768,768]{1,0:T(8,128)S(1)} %fusion.61, bf16[32,768,128]{1,2,0:T(8,128)(2,1)} %bitcast.79, bf16[768,32,128]{2,0,1:T(8,128)(2,1)} %copy.45), kind=kOutput, calls=%fused_computation.1 | convolution fusion | flops 4869586944 | bytes 52690944 | tf_op jit(solution)/shard_map/hta,hsa->hts/dot_general | solution.py:45
  135.6 93.9 %all-gather.3.cloned.1.call-done = bf16[16,4096,128]{2,1,0:T(8,128)(2,1)} async-done(((bf16[1,4096,128]{2,1,0:T(8,128)(2,1)}), bf16[16,4096,128]{2,1,0:T(8,128)(2,1)}) %all-gather.3.cloned.1.call-update) | async-done | bytes 16777232 | tf_op jit(solution)/shard_map/all_gather | solution.py:36
  229.5 17.1 %fusion.18 = f32[1,4096,128]{2,0,1:T(1,128)} fusion(bf16[16,4096,128]{2,1,0:T(8,128)(2,1)} %all-gather.3.cloned.1.call-done, bf16[16]{0:T(256)(128)(2,1)S(1)} %get-tuple-element.18, bf16[]{:T(256)} %convert_element_type.91, s32[]{:T(128)S(6)} %axis_index.19), kind=kOutput, calls=%fused_computation.20 | convolution fusion | flops 16777296 | bytes 18874406 | tf_op jit(solution)/shard_map/n,nab->ab/dot_general | solution.py:42
  246.6 1.7 convert_element_type.94
  248.3 1.3 copy.50
  249.7 0.0 copy-start
  249.7 24.4 %fusion.25 = (f32[768]{0:T(1024)S(1)}, f32[32,768,128]{1,2,0:T(8,128)}) fusion(bf16[32,128,128]{1,2,0:T(8,128)(2,1)} %copy.50, bf16[32,768,128]{1,2,0:T(8,128)(2,1)} %bitcast.83, bf16[32,768,128]{2,1,0:T(8,128)(2,1)} %broadcast_multiply_fusion.1, bf16[32,768,768]{2,1,0:T(8,128)(2,1)} %multiply_convert_fusion.1), kind=kOutput, calls=%fused_computation.31 | convolution fusion | flops 5746195456 | bytes 63966208 | tf_op jit(solution)/shard_map/htk,hkb->htb/dot_general | solution.py:48
  274.1 0.0 copy-done
  274.1 7.4 %fusion.22 = f32[768]{0:T(1024)S(1)} fusion(f32[32,768,128]{1,2,0:T(8,128)} %get-tuple-element.31, bf16[768,4096]{0,1:T(8,128)(2,1)} %copy.51, f32[4096]{0:T(1024)S(1)} %copy-done), kind=kLoop, calls=%fused_computation.27 | loop fusion | flops 12582144 | bytes 18893824 | tf_op jit(solution)/shard_map/reduce_sum | solution.py:57
  281.5 2.5 all-reduce.2
  284.0 13.2 %fusion.24 = (bf16[768,4096]{0,1:T(8,128)(2,1)}, bf16[768,4096]{0,1:T(8,128)(2,1)}) fusion(f32[32,768,128]{1,2,0:T(8,128)} %get-tuple-element.31, bf16[768,4096]{0,1:T(8,128)(2,1)} %copy.51, f32[768]{0:T(1024)S(1)} %get-tuple-element.22, f32[4096]{0:T(1024)S(1)} %copy-done, f32[768]{0:T(1024)S(1)} %get-tuple-element.23), kind=kLoop, calls=%fused_computation.29 | loop fusion | flops 28311552 | bytes 31479808 | tf_op jit(solution)/shard_map/convert_element_type | solution.py:63
  297.3 8.6 %copy.52 = bf16[768,32,128]{2,0,1:T(8,128)(2,1)} copy(bf16[768,32,128]{0,2,1:T(8,128)(2,1)} %bitcast.88) | data formatting | bytes 12582912 | tf_op jit(solution)/shard_map/reshape | solution.py:64
  305.9 7.5 %convolution_convert_fusion = bf16[32,128,128]{2,1,0:T(8,128)(2,1)} fusion(bf16[32,768,128]{2,1,0:T(8,128)(2,1)} %broadcast_multiply_fusion.1, bf16[768,32,128]{2,0,1:T(8,128)(2,1)} %copy.52), kind=kOutput, calls=%fused_computation.59 | convolution fusion | flops 805830656 | bytes 13631488 | tf_op jit(solution)/shard_map/hta,htb->hab/dot_general | solution.py:65
  313.4 0.0 all-gather.5.cloned.1.call-update
  313.4 10.3 %multiply_bitcast_fusion = (bf16[32,128,768]{2,1,0:T(8,128)(2,1)}, bf16[32,128,768]{2,1,0:T(8,128)(2,1)}) fusion(bf16[768,32,128]{0,2,1:T(8,128)(2,1)} %bitcast.80, bf16[768]{0:T(1024)(128)(2,1)S(1)} %get-tuple-element.24, bf16[768,32,128]{0,2,1:T(8,128)(2,1)} %bitcast.84), kind=kLoop, calls=%fused_computation.45 | loop fusion | flops 6291456 | bytes 25167360 | tf_op jit(solution)/shard_map/mul | solution.py:30
  323.7 6.0 %broadcast_multiply_fusion = bf16[32,768,128]{2,1,0:T(8,128)(2,1)} fusion(bf16[768]{0:T(1024)(128)(2,1)S(1)} %get-tuple-element.25, bf16[768,32,128]{2,0,1:T(8,128)(2,1)} %copy.52), kind=kLoop, calls=%fused_computation.53 | loop fusion | flops 3145728 | bytes 12584448 | tf_op jit(solution)/shard_map/mul | solution.py:83
  329.7 19.3 %multiply_convert_fusion = bf16[32,768,768]{2,1,0:T(8,128)(2,1)} fusion(f32[768,768]{1,0:T(8,128)S(1)} %fusion.61, bf16[32,768,128]{1,2,0:T(8,128)(2,1)} %bitcast.85, bf16[768,32,128]{2,0,1:T(8,128)(2,1)} %copy.52), kind=kOutput, calls=%fused_computation | convolution fusion | flops 4869586944 | bytes 52690944 | tf_op jit(solution)/shard_map/htb,hsb->hts/dot_general | solution.py:78
  349.1 23.3 %fusion.50 = bf16[32,768,128]{1,2,0:T(8,128)(2,1)} fusion(bf16[32,128,128]{1,2,0:T(8,128)(2,1)S(1)} %bitcast.95, bf16[32,768,128]{1,2,0:T(8,128)(2,1)} %bitcast.81, bf16[32,768,128]{2,1,0:T(8,128)(2,1)} %broadcast_multiply_fusion, bf16[32,768,768]{2,1,0:T(8,128)(2,1)} %multiply_convert_fusion), kind=kOutput, calls=%fused_computation.51 | convolution fusion | flops 5743050752 | bytes 57671680 | tf_op jit(solution)/shard_map/htk,hka->hta/dot_general | solution.py:81
  372.4 8.6 %copy.59 = bf16[768,4096]{1,0:T(8,128)(2,1)} copy(bf16[768,4096]{0,1:T(8,128)(2,1)} %bitcast.92) | data formatting | bytes 12582912
  381.0 0.0 copy-start.2
  381.0 9.0 %copy.58 = bf16[768,4096]{1,0:T(8,128)(2,1)} copy(bf16[768,4096]{0,1:T(8,128)(2,1)} %get-tuple-element.21) | data formatting | bytes 12582912
  390.0 113.3 %all-gather.5.cloned.1.call-done = bf16[16,4096,128]{2,1,0:T(8,128)(2,1)} async-done(((bf16[1,4096,128]{2,1,0:T(8,128)(2,1)}), bf16[16,4096,128]{2,1,0:T(8,128)(2,1)}) %all-gather.5.cloned.1.call-update) | async-done | bytes 16777232 | tf_op jit(solution)/shard_map/all_gather | solution.py:69
  503.4 0.0 copy-done.2
  503.4 15.8 %fusion.16 = f32[1,4096,128]{2,0,1:T(1,128)S(1)} fusion(bf16[16,4096,128]{2,1,0:T(8,128)(2,1)} %all-gather.5.cloned.1.call-done, bf16[16]{0:T(256)(128)(2,1)S(1)} %copy-done.2, bf16[]{:T(256)} %convert_element_type.90, s32[]{:T(128)S(6)} %axis_index.19), kind=kOutput, calls=%fused_computation.18 | convolution fusion | flops 16777296 | bytes 18874406 | tf_op jit(solution)/shard_map/n,nab->ab/dot_general | solution.py:75
  519.2 0.1 convert_element_type.103
  519.3 21.5 %fusion.40 = bf16[32,768,128]{1,2,0:T(8,128)(2,1)} fusion(bf16[32,128,128]{2,1,0:T(8,128)(2,1)S(1)} %bitcast.96, bf16[32,768,128]{2,1,0:T(8,128)(2,1)} %bitcast.77, bf16[32,128,768]{2,1,0:T(8,128)(2,1)} %get-tuple-element.28, bf16[32,768,768]{2,1,0:T(8,128)(2,1)} %multiply_convert_fusion.1), kind=kOutput, calls=%fused_computation.49 | convolution fusion | flops 5743050752 | bytes 57671680 | tf_op jit(solution)/shard_map/hks,hkb->hsb/dot_general | solution.py:93
  540.8 8.6 %copy.61 = bf16[768,4096]{1,0:T(8,128)(2,1)} copy(bf16[768,4096]{0,1:T(8,128)(2,1)} %bitcast.93) | data formatting | bytes 12582912
  549.4 0.7 copy.55
  550.0 21.1 %fusion.45 = bf16[32,768,128]{1,2,0:T(8,128)(2,1)} fusion(bf16[32,128,128]{2,1,0:T(8,128)(2,1)S(1)} %copy.55, bf16[32,768,128]{2,1,0:T(8,128)(2,1)} %bitcast.86, bf16[32,128,768]{2,1,0:T(8,128)(2,1)} %get-tuple-element.29, bf16[32,768,768]{2,1,0:T(8,128)(2,1)} %multiply_convert_fusion), kind=kOutput, calls=%fused_computation.50 | convolution fusion | flops 5743050752 | bytes 57671680 | tf_op jit(solution)/shard_map/hks,hka->hsa/dot_general | solution.py:87
  571.1 8.6 %copy.60 = bf16[768,4096]{1,0:T(8,128)(2,1)} copy(bf16[768,4096]{0,1:T(8,128)(2,1)} %bitcast.91) | data formatting | bytes 12582912
  (3 shorter events, 0.0 us)
Async XLA Ops:
  7.2 222.4 %all-gather.3.cloned.1.call-start = ((), (), s32[]{:S(2)}) async-start(), calls=%async_computation | async-start | bytes 17825792 | tf_op jit(solution)/shard_map/all_gather | solution.py:36
  17.2 8.6 %copy-start.1 = (s32[768]{0:T(1024)S(1)}, s32[768]{0:T(1024)}, u32[]{:S(2)}) copy-start(s32[768]{0:T(1024)} %param.11) | copy-start | bytes 9220
  27.1 8.8 %copy-start.3 = (u32[32]{0:T(128)S(1)}, u32[32]{0:T(128)}, u32[]{:S(2)}) copy-start(u32[32]{0:T(128)} %constant.16) | copy-start | bytes 388
  34.5 468.8 %all-gather.5.cloned.1.call-start = ((), (), s32[]{:S(2)}) async-start(), calls=%async_computation.1 | async-start | bytes 17825792 | tf_op jit(solution)/shard_map/all_gather | solution.py:69
  249.7 24.4 %copy-start = (f32[4096]{0:T(1024)S(1)}, f32[4096]{0:T(1024)}, u32[]{:S(2)}) copy-start(f32[4096]{0:T(1024)} %param.10) | copy-start | bytes 49156
  381.0 122.4 %copy-start.2 = (bf16[16]{0:T(256)(128)(2,1)S(1)}, bf16[16]{0:T(256)(128)(2,1)}, u32[]{:S(2)}) copy-start(bf16[16]{0:T(256)(128)(2,1)} %get-tuple-element.19) | copy-start | bytes 100
Sparse Core Ops, SparseCore 0:
  34.6 194.8 all-gather.2
  313.5 189.7 all-gather.4
where the time goes:
time: 594 us; the launch traced here: 587 us
  waiting for transfers between devices  207 us (35%)
  matrix products  178 us (30%)
  local copies, waits for them, and re-layouts  91.9 us (15%)
  blocking collectives  47.7 us (8%)
  other arithmetic  46.3 us (8%)
  between operations  15.6 us (3%)
    all_gather x1, waiting for transfers between devices, shards(): lax.all_gather(own_reverse.reshape(1, heads_here * HD, HD), 'ctx', axis=0...  113 us
    all_gather x1, waiting for transfers between devices, shards(): lax.all_gather(own_state.reshape(1, heads_here * HD, HD), 'ctx', axis=0,...  93.9 us
    unnamed x21, local copies, waits for them, and re-layouts  71.4 us
    unnamed x1, blocking collectives  45.2 us
    dot_general x2, matrix products, shards(): jnp.einsum('n,nab->ab', weights, blocks, preferred_element_type=jnp.float32)  32.9 us
    dot_general x1, matrix products, shards(): jnp.einsum('htk,hkb->htb', jnp.concatenate([scores, query_first], axis=2)...  24.4 us
    dot_general x1, matrix products, shards(): jnp.einsum('htk,hka->hta', jnp.concatenate([dscores, delta_heads * first_...  23.3 us
    dot_general x1, matrix products, shards(): jnp.einsum('hks,hkb->hsb', jnp.concatenate([scores, key_last.transpose(0,...  21.5 us
  transfers between devices with their start and end apart: 2, of which 2 were waited for; matrix products, arithmetic and copies ran while one was open for 22% of the time, Pallas kernels for 0%

commit v1 on v0

v1 whole, which is shorter than its diff:
```python
import functools

import jax
import jax.numpy as jnp
from jax import lax
from jax.experimental import pallas as pl
from jax.experimental.pallas import tpu as pltpu
from jax.sharding import PartitionSpec as P

HEADS = 64
HD = 128
NORM_EPS = 1e-06
MEMBERS = 4
CHUNKS = 2
ROWS = 256
F32 = jnp.float32
BF16 = jnp.bfloat16


def dot_nn(a, b):
    return lax.dot_general(a, b, (((1,), (0,)), ((), ())), preferred_element_type=F32)


def dot_nt(a, b):
    return lax.dot_general(a, b, (((1,), (1,)), ((), ())), preferred_element_type=F32)


def dot_tn(a, b):
    return lax.dot_general(a, b, (((0,), (0,)), ((), ())), preferred_element_type=F32)


def state_kernel(k_ref, v_ref, last_ref, state_ref):
    for h in range(k_ref.shape[1] // HD):
        cols = slice(h * HD, (h + 1) * HD)
        state_ref[cols, :] = dot_tn(k_ref[:, cols] * last_ref[...], v_ref[:, cols]).astype(BF16)


def exchange_kernel(groups, reverse, state_ref, tag_ref, out_ref, got, tags, chain_in, chain_out,
                    chain_tag, sends, back, sem_a, sem_b, sem_c, sem_d, sem_e):
    me = lax.axis_index("ctx")
    group, member = me // MEMBERS, me % MEMBERS
    step = -1 if reverse else 1
    place = groups - 1 - group if reverse else group
    have, need = (0, 1) if reverse else (1, 0)
    tail = 0 if reverse else MEMBERS - 1
    part = state_ref.shape[0] // MEMBERS
    piece = part // CHUNKS
    ahead = (group + step + groups) % groups * MEMBERS + member
    behind = (group - step + groups) % groups * MEMBERS + member

    barrier = pltpu.get_barrier_semaphore()
    for r in range(1, MEMBERS):
        pl.semaphore_signal(barrier, inc=1, device_id={"ctx": group * MEMBERS + (member + r) % MEMBERS})
    pl.semaphore_signal(barrier, inc=1, device_id={"ctx": ahead})
    pl.semaphore_signal(barrier, inc=1, device_id={"ctx": behind})
    pl.semaphore_wait(barrier, MEMBERS + 1)

    def scatter(m, slot):
        return pltpu.make_async_remote_copy(
            src_ref=state_ref.at[pl.ds(m * part, part)], dst_ref=got.at[slot],
            send_sem=sem_a.at[0, m], recv_sem=sem_a.at[1, slot], device_id={"ctx": group * MEMBERS + m})

    def label(m, slot):
        return pltpu.make_async_remote_copy(
            src_ref=tag_ref, dst_ref=tags.at[slot],
            send_sem=sem_b.at[0, m], recv_sem=sem_b.at[1, slot], device_id={"ctx": group * MEMBERS + m})

    def chain(c):
        return pltpu.make_async_remote_copy(
            src_ref=chain_out.at[c], dst_ref=chain_in.at[c],
            send_sem=sem_c.at[0, c], recv_sem=sem_c.at[1, c], device_id={"ctx": ahead})

    def chain_label():
        return pltpu.make_async_remote_copy(
            src_ref=tags.at[tail], dst_ref=chain_tag,
            send_sem=sem_d.at[0], recv_sem=sem_d.at[1], device_id={"ctx": ahead})

    def give(m, slot, c):
        return pltpu.make_async_remote_copy(
            src_ref=sends.at[m, c], dst_ref=back.at[slot, c],
            send_sem=sem_e.at[0, m, c], recv_sem=sem_e.at[1, slot, c], device_id={"ctx": group * MEMBERS + m})

    for m in range(MEMBERS):
        @pl.when(m != member)
        def _(m=m):
            label(m, member).start()
            scatter(m, member).start()

        @pl.when(m == member)
        def _(m=m):
            tags[m] = tag_ref[...]
            got[m] = state_ref[m * part:(m + 1) * part, :]

    @pl.when(place == 0)
    def _():
        chain_tag[...] = jnp.full_like(chain_tag, -1.0)
        chain_in[...] = jnp.zeros_like(chain_in)

    for m in range(MEMBERS):
        @pl.when(m != member)
        def _(m=m):
            label(m, m).wait_recv()

    @pl.when(place < groups - 1)
    def _():
        chain_label().start()

    for m in range(MEMBERS):
        @pl.when(m != member)
        def _(m=m):
            scatter(m, m).wait_recv()

    @pl.when(place > 0)
    def _():
        chain_label().wait_recv()

    def equal(a, b):
        return (a == b).astype(F32)

    haves = [tags[m, have:have + 1, :] for m in range(MEMBERS)]
    needs = [tags[m, need:need + 1, :] for m in range(MEMBERS)]
    before = chain_tag[have:have + 1, :]
    order = range(MEMBERS - 1, -1, -1) if reverse else range(MEMBERS)
    for c in range(CHUNKS):
        rows = slice(c * piece, (c + 1) * piece)
        total = jnp.zeros((piece, HD), F32)
        for m in range(MEMBERS):
            total += equal(haves[m], haves[tail]) * got[m, rows, :].astype(F32)

        @pl.when(place > 0)
        def _(c=c):
            chain(c).wait_recv()

        arrived = chain_in[c].astype(F32)
        chain_out[c] = (total + equal(before, haves[tail]) * arrived).astype(BF16)

        @pl.when(place < groups - 1)
        def _(c=c):
            chain(c).start()

        done = []
        for m in order:
            own = equal(before, needs[m]) * arrived
            for j in done:
                own += equal(haves[j], needs[m]) * got[j, rows, :].astype(F32)
            done.append(m)
            own = own.astype(BF16)

            @pl.when(m != member)
            def _(m=m, c=c, own=own):
                sends[m, c] = own
                give(m, member, c).start()

            @pl.when(m == member)
            def _(m=m, c=c, own=own):
                back[m, c] = own

    for m in range(MEMBERS):
        for c in range(CHUNKS):
            @pl.when(m != member)
            def _(m=m, c=c):
                give(m, m, c).wait_recv()
            out_ref[m * part + c * piece:m * part + (c + 1) * piece, :] = back[m, c]

    for m in range(MEMBERS):
        @pl.when(m != member)
        def _(m=m):
            label(m, member).wait_send()
            scatter(m, member).wait_send()
            for c in range(CHUNKS):
                give(m, member, c).wait_send()

    @pl.when(place < groups - 1)
    def _():
        chain_label().wait_send()
        for c in range(CHUNKS):
            chain(c).wait_send()


def exchange(state, tag, blocks, reverse):
    groups = blocks // MEMBERS
    part = state.shape[0] // MEMBERS
    piece = part // CHUNKS
    vmem = pl.BlockSpec(memory_space=pltpu.VMEM)
    return pl.pallas_call(
        functools.partial(exchange_kernel, groups, reverse),
        out_shape=jax.ShapeDtypeStruct(state.shape, BF16),
        in_specs=[vmem, vmem],
        out_specs=vmem,
        scratch_shapes=[
            pltpu.VMEM((MEMBERS, part, HD), BF16),
            pltpu.VMEM((MEMBERS, 8, HD), F32),
            pltpu.VMEM((CHUNKS, piece, HD), BF16),
            pltpu.VMEM((CHUNKS, piece, HD), BF16),
            pltpu.VMEM((8, HD), F32),
            pltpu.VMEM((MEMBERS, CHUNKS, piece, HD), BF16),
            pltpu.VMEM((MEMBERS, CHUNKS, piece, HD), BF16),
            pltpu.SemaphoreType.DMA((2, MEMBERS)),
            pltpu.SemaphoreType.DMA((2, MEMBERS)),
            pltpu.SemaphoreType.DMA((2, CHUNKS)),
            pltpu.SemaphoreType.DMA((2,)),
            pltpu.SemaphoreType.DMA((2, MEMBERS, CHUNKS)),
        ],
        compiler_params=pltpu.CompilerParams(collective_id=1 if reverse else 0, has_side_effects=True,
                                             vmem_limit_bytes=16 * 2**20),
        name="exchange_back" if reverse else "exchange_on",
    )(state, tag)


def forward_kernel(q_ref, k_ref, v_ref, og_ref, gain_ref, inc_ref, mask_ref, first_ref,
                   att_ref, square_ref, cross_ref):
    @pl.when(pl.program_id(0) == 0)
    def _():
        square_ref[...] = jnp.zeros_like(square_ref)
        cross_ref[...] = jnp.zeros_like(cross_ref)

    tokens = q_ref.shape[0]
    for h in range(q_ref.shape[1] // HD):
        cols = slice(h * HD, (h + 1) * HD)
        for start in range(0, tokens, ROWS):
            stop = start + ROWS
            rows = slice(start, stop)
            q = q_ref[rows, cols]
            scores = dot_nt(q, k_ref[:stop, cols]).astype(BF16) * mask_ref[rows, :stop]
            att = dot_nn(scores, v_ref[:stop, cols])
            att += dot_nn(q * first_ref[rows, :], inc_ref[cols, :])
            att_ref[rows, cols] = att
            square_ref[rows, :] += att * att
            cross_ref[rows, :] += gain_ref[:, cols] * og_ref[rows, cols].astype(F32) * att


def delta_kernel(att_ref, og_ref, q_ref, gain_ref, inverse_ref, weight_ref, first_ref,
                 normed_ref, delta_ref, state_ref):
    for h in range(q_ref.shape[1] // HD):
        cols = slice(h * HD, (h + 1) * HD)
        att = att_ref[:, cols]
        gain = gain_ref[:, cols]
        inverse = inverse_ref[...]
        normed_ref[:, cols] = (att * inverse * gain).astype(BF16)
        delta = (inverse * (gain * og_ref[:, cols].astype(F32)) - att * weight_ref[...]).astype(BF16)
        delta_ref[:, cols] = delta
        state_ref[cols, :] = dot_tn(q_ref[:, cols] * first_ref[...], delta).astype(BF16)


def backward_kernel(q_ref, k_ref, v_ref, d_ref, inc_ref, out_ref, mask_ref, first_ref, last_ref,
                    gq_ref, gk_ref, gv_ref):
    tokens = q_ref.shape[0]
    for h in range(q_ref.shape[1] // HD):
        cols = slice(h * HD, (h + 1) * HD)
        grad_query = dot_nt(d_ref[:, cols] * first_ref[...], inc_ref[cols, :])
        pieces = [grad_query[r:r + ROWS] for r in range(0, tokens, ROWS)]
        for start in range(0, tokens, ROWS):
            rows = slice(start, start + ROWS)
            k, v = k_ref[rows, cols], v_ref[rows, cols]
            q, d = q_ref[start:, cols], d_ref[start:, cols]
            mask = mask_ref[rows, start:]
            last = last_ref[rows, :]
            scores = dot_nt(k, q).astype(BF16) * mask
            dscores = dot_nt(v, d).astype(BF16) * mask
            gv_ref[rows, cols] = (dot_nn(scores, d) + dot_nn(k * last, out_ref[cols, :])).astype(BF16)
            gk_ref[rows, cols] = (dot_nn(dscores, q) + dot_nt(v * last, out_ref[cols, :])).astype(BF16)
            more = dot_tn(dscores, k)
            for i in range(start // ROWS, tokens // ROWS):
                at = i * ROWS - start
                pieces[i] = pieces[i] + more[at:at + ROWS]
        for i, piece in enumerate(pieces):
            gq_ref[i * ROWS:(i + 1) * ROWS, cols] = piece.astype(BF16)


def shards(blocks, queries, keys, values, out_grad, gain, doc_ids):
    tokens, width = queries.shape
    heads = width // HD
    width_all = HEADS * HD
    position = jnp.arange(tokens)
    same = doc_ids[:, None] == doc_ids[None, :]
    mask = (same & (position[:, None] >= position[None, :])).astype(BF16)
    mask_t = (same & (position[:, None] <= position[None, :])).astype(BF16)
    first_doc, last_doc = doc_ids[0], doc_ids[tokens - 1]
    first_rows = jnp.broadcast_to((doc_ids == first_doc).astype(BF16)[:, None], (tokens, HD))
    last_rows = jnp.broadcast_to((doc_ids == last_doc).astype(BF16)[:, None], (tokens, HD))
    tag = jnp.where(jnp.arange(8)[:, None] == 0, first_doc, last_doc).astype(F32)
    tag = jnp.broadcast_to(tag, (8, HD))
    gain = gain[None, :]

    each = 2
    wide = each * HD
    grid = (heads // each,)
    head_cols = pl.BlockSpec((tokens, wide), lambda i: (0, i))
    gain_cols = pl.BlockSpec((1, wide), lambda i: (0, i))
    head_state = pl.BlockSpec((wide, HD), lambda i: (i, 0))
    whole = pl.BlockSpec((tokens, HD), lambda i: (0, 0))
    whole_mask = pl.BlockSpec((tokens, tokens), lambda i: (0, 0))
    state_shape = jax.ShapeDtypeStruct((width, HD), BF16)
    flat_shape = jax.ShapeDtypeStruct((tokens, width), BF16)
    sums_shape = jax.ShapeDtypeStruct((tokens, HD), F32)
    params = pltpu.CompilerParams(vmem_limit_bytes=40 * 2**20)

    own_state = pl.pallas_call(
        state_kernel, grid=grid, in_specs=[head_cols, head_cols, whole], out_specs=head_state,
        out_shape=state_shape, compiler_params=params, name="block_state",
    )(keys, values, last_rows)
    incoming = exchange(own_state, tag, blocks, False)
    attended, squares, crosses = pl.pallas_call(
        forward_kernel, grid=grid,
        in_specs=[head_cols, head_cols, head_cols, head_cols, gain_cols, head_state, whole_mask, whole],
        out_specs=[head_cols, whole, whole],
        out_shape=[jax.ShapeDtypeStruct((tokens, width), F32), sums_shape, sums_shape],
        compiler_params=params, name="attend",
    )(queries, keys, values, out_grad, gain, incoming, mask, first_rows)
    square_sum, cross_sum = lax.psum((jnp.sum(squares, axis=1), jnp.sum(crosses, axis=1)), "tp")
    inverse = lax.rsqrt(square_sum / width_all + NORM_EPS)
    weight = inverse**3 * cross_sum / width_all
    inverse = jnp.broadcast_to(inverse[:, None], (tokens, HD))
    weight = jnp.broadcast_to(weight[:, None], (tokens, HD))
    normed, delta, own_reverse = pl.pallas_call(
        delta_kernel, grid=grid,
        in_specs=[head_cols, head_cols, head_cols, gain_cols, whole, whole, whole],
        out_specs=[head_cols, head_cols, head_state],
        out_shape=[flat_shape, flat_shape, state_shape],
        compiler_params=params, name="delta",
    )(attended, out_grad, queries, gain, inverse, weight, first_rows)
    outgoing = exchange(own_reverse, tag, blocks, True)
    grad_query, grad_key, grad_value = pl.pallas_call(
        backward_kernel, grid=grid,
        in_specs=[head_cols] * 4 + [head_state] * 2 + [whole_mask, whole, whole],
        out_specs=[head_cols] * 3, out_shape=[flat_shape] * 3,
        compiler_params=params, name="grads",
    )(queries, keys, values, delta, incoming, outgoing, mask_t, first_rows, last_rows)
    return normed, grad_query, grad_key, grad_value


def solution(mesh):
    in_specs = (P("ctx", "tp"), P("ctx", "tp"), P("ctx", "tp"), P("ctx", "tp"), P("tp"), P("ctx"))
    out_specs = (P("ctx", "tp"), P("ctx", "tp"), P("ctx", "tp"), P("ctx", "tp"))
    return jax.shard_map(functools.partial(shards, mesh.shape["ctx"]), mesh=mesh, in_specs=in_specs,
                         out_specs=out_specs, check_vma=False)
```

time: 594 us -> 200 us (0.34); the launches traced: 587 us -> 199 us
  waiting for transfers between devices: 207 us -> 0 us
  Pallas kernels: 0 us -> 181 us
  matrix products: 178 us -> 0 us
  local copies, waits for them, and re-layouts: 91.9 us -> 10.5 us
  blocking collectives: 47.7 us -> 2.5 us
  other arithmetic: 46.3 us -> 4.19 us
  between operations: 15.6 us -> 0.82 us
    all_gather x2 -> x0, waiting for transfers between devices: 207 us -> none  [the longest x1 113 us: shards(): lax.all_gather(own_reverse.reshape(1, heads_here * HD, HD), 'ctx', axis=0...]
    pallas_call x0 -> x6, Pallas kernels: none -> 181 us  [the longest x2 84.9 us: exchange(): pl.pallas_call(functools.partial(exchange_kernel, groups, reverse), out_s...]
    dot_general x10 -> x0, matrix products: 178 us -> none  [the longest x2 32.9 us: shards(): jnp.einsum('n,nab->ab', weights, blocks, preferred_element_type=jnp.float32)]
    unnamed x21 -> x18, local copies, waits for them, and re-layouts: 71.4 us -> 8.4 us
    unnamed x1 -> x0, blocking collectives: 45.2 us -> none
    mul x3 -> x0, other arithmetic: 22.3 us -> none  [the longest x1 10.3 us: shards(): key_last = key_heads * last_rows]
    reshape x2 -> x0, local copies, waits for them, and re-layouts: 17.1 us -> none  [the longest x1 8.61 us: shards(): delta_heads = delta.reshape(tokens_here, heads_here, HD).transpose(1, 0, 2)]
    convert_element_type x5 -> x3, other arithmetic: 16.6 us -> 3.83 us  [the longest x1 1.99 us: shards(): (doc_ids == first_doc).astype(BF16)[:, None]]
  transfers between devices with their start and end apart: 2 -> 0, of which waited for: 2 -> 0; matrix products, arithmetic and copies ran while one was open for 22% -> 0% of each run, Pallas kernels for 0% -> 0%
where the time goes in v1:
time: 200 us; the launch traced here: 199 us
  Pallas kernels  181 us (90%)
  local copies, waits for them, and re-layouts  10.5 us (5%)
  other arithmetic  4.19 us (2%)
  blocking collectives  2.5 us (1%)
    pallas_call x2, Pallas kernels, exchange(): pl.pallas_call(functools.partial(exchange_kernel, groups, reverse), out_s...  84.9 us
    pallas_call x1, Pallas kernels, shards(): pl.pallas_call(backward_kernel, grid=grid, in_specs=[head_cols] * 4 + [he...  45.9 us
    pallas_call x1, Pallas kernels, shards(): pl.pallas_call(forward_kernel, grid=grid, in_specs=[head_cols, head_cols,...  25.2 us
    pallas_call x1, Pallas kernels, shards(): pl.pallas_call(delta_kernel, grid=grid, in_specs=[head_cols, head_cols, h...  18.1 us
    unnamed x18, local copies, waits for them, and re-layouts  8.4 us
    pallas_call x1, Pallas kernels, shards(): pl.pallas_call(state_kernel, grid=grid, in_specs=[head_cols, head_cols, w...  6.84 us

profile of v1, /device:TPU:0, one launch (start us, length us, event | category | flops | bytes accessed | tf_op | source)
XLA Modules:
  0.0 198.8 jit_solution(3053272205278142061)
XLA Ops:
  0.6 1.3 fusion.5
  2.0 1.3 fusion.4
  3.3 2.0 compare_convert_fusion
  5.3 0.1 broadcast_in_dim.24.tag_ref
  5.3 0.2 broadcast_in_dim.25.first_ref
  5.5 0.0 slice-start
  5.5 0.2 broadcast_in_dim.21.last_ref
  5.7 0.0 copy-start
  5.7 2.9 %copy-done = bf16[768,4096]{1,0:T(8,128)(2,1)S(1)} copy-done((bf16[768,4096]{1,0:T(8,128)(2,1)S(1)}, bf16[768,4096]{1,0:T(8,128)(2,1)}, u32[]{:S(2)}) %copy-start) | copy-done | bytes 6291480
  8.6 0.0 copy-start.1
  8.6 2.8 %copy-done.1 = bf16[768,4096]{1,0:T(8,128)(2,1)S(1)} copy-done((bf16[768,4096]{1,0:T(8,128)(2,1)S(1)}, bf16[768,4096]{1,0:T(8,128)(2,1)}, u32[]{:S(2)}) %copy-start.1) | copy-done | bytes 6291480
  11.4 0.0 copy-start.4
  11.4 0.0 slice-start.1
  11.4 0.0 copy-start.3
  11.4 6.8 %block_state.1.state_ref = bf16[4096,128]{1,0:T(8,128)(2,1)S(1)} custom-call(bf16[768,4096]{1,0:T(8,128)(2,1)S(1)} %copy-done, bf16[768,4096]{1,0:T(8,128)(2,1)S(1)} %copy-done.1, bf16[768,128]{1,0:T(8,128)(2,1)S(1)} %broadcast_in_dim.21.last_ref), custom_call_target="tpu_custom_call" | custom-call | tf_op jit(solution)/shard_map/block_state/pallas_call | solution.py:298
  18.3 31.6 %exchange_on.1.inc_ref = bf16[4096,128]{1,0:T(8,128)(2,1)S(1)} custom-call(bf16[4096,128]{1,0:T(8,128)(2,1)S(1)} %block_state.1.state_ref, f32[8,128]{1,0:T(8,128)S(1)} %broadcast_in_dim.24.tag_ref), custom_call_target="tpu_custom_call" | custom-call | tf_op jit(solution)/shard_map/exchange_on/pallas_call | solution.py:185
  49.8 0.0 copy-done.4
  49.9 0.5 fusion.1
  50.4 0.0 slice-done
  50.4 0.0 slice-done.1
  50.4 0.0 copy-done.3
  50.4 25.2 %attend.1 = (f32[768,4096]{1,0:T(8,128)}, f32[768,128]{1,0:T(8,128)S(1)}, f32[768,128]{1,0:T(8,128)S(1)}) custom-call(bf16[768,4096]{1,0:T(8,128)(2,1)S(1)} %bitcast.4, bf16[768,4096]{1,0:T(8,128)(2,1)} %k_ref.5, bf16[768,4096]{1,0:T(8,128)(2,1)} %v_ref.5, bf16[768,4096]{1,0:T(8,128)(2,1)} %og_ref.3, f32[1,4096]{1,0:T(1,128)S(1)} %bitcast.7, ...), custom_call_target="tpu_custom_call" | custom-call | tf_op jit(solution)/shard_map/attend/pallas_call | solution.py:303
  75.6 0.2 reduce_sum.18
  75.8 0.2 reduce_sum.19
  76.0 2.5 %all-reduce = (f32[768]{0:T(1024)S(1)}, f32[768]{0:T(1024)S(1)}) all-reduce(f32[768]{0:T(1024)S(1)} %reduce_sum.18, f32[768]{0:T(1024)S(1)} %reduce_sum.19), channel_id=1, replica_groups=mesh['ctx'=16,'tp'=2] {'tp'}, use_global_device_ids=true, to_apply=%region_1.2 | all-reduce | flops 1536 | bytes 12288 | tf_op jit(solution)/shard_map/psum | solution.py:310
  78.5 0.2 broadcast_in_dim.27.weight_ref
  78.7 0.0 slice-start.2
  78.7 0.2 broadcast_in_dim.26.inverse_ref
  78.8 0.0 slice-start.3
  78.9 18.1 %delta.1 = (bf16[768,4096]{1,0:T(8,128)(2,1)}, bf16[768,4096]{1,0:T(8,128)(2,1)S(1)}, bf16[4096,128]{1,0:T(8,128)(2,1)S(1)}) custom-call(f32[768,4096]{1,0:T(8,128)} %get-tuple-element.13.att_ref, bf16[768,4096]{1,0:T(8,128)(2,1)} %og_ref.3, bf16[768,4096]{1,0:T(8,128)(2,1)} %q_ref.5, f32[1,4096]{1,0:T(1,128)S(1)} %bitcast.8, ...), custom_call_target="tpu_custom_call" | custom-call | tf_op jit(solution)/shard_map/delta/pallas_call | solution.py:315
  96.9 0.0 copy-start.2
  96.9 2.6 %copy-done.2 = bf16[768,4096]{1,0:T(8,128)(2,1)} copy-done((bf16[768,4096]{1,0:T(8,128)(2,1)}, bf16[768,4096]{1,0:T(8,128)(2,1)S(1)}, u32[]{:S(2)}) %copy-start.2) | copy-done | bytes 6291480
  99.6 53.3 %exchange_back.1.out_ref = bf16[4096,128]{1,0:T(8,128)(2,1)S(1)} custom-call(bf16[4096,128]{1,0:T(8,128)(2,1)S(1)} %get-tuple-element.18.state_ref, f32[8,128]{1,0:T(8,128)S(1)} %broadcast_in_dim.24.tag_ref), custom_call_target="tpu_custom_call" | custom-call | tf_op jit(solution)/shard_map/exchange_back/pallas_call | solution.py:185
  152.9 0.0 slice-done.2
  152.9 0.0 slice-done.3
  152.9 45.9 %grads.1 = (bf16[768,4096]{1,0:T(8,128)(2,1)}, bf16[768,4096]{1,0:T(8,128)(2,1)}, bf16[768,4096]{1,0:T(8,128)(2,1)}) custom-call(bf16[768,4096]{1,0:T(8,128)(2,1)S(1)} %bitcast.6, bf16[768,4096]{1,0:T(8,128)(2,1)} %k_ref.5, bf16[768,4096]{1,0:T(8,128)(2,1)} %v_ref.5, bf16[768,4096]{1,0:T(8,128)(2,1)} %copy-done.2, bf16[4096,128]{1,0:T(8,128)(2,1)S(1)} %exchange_on.1.inc_ref, ...), custom_call_target="tpu_custom_call" | custom-call | tf_op jit(solution)/shard_map/grads/pallas_call | solution.py:323
  (3 shorter events, 0.0 us)
Async XLA Ops:
  5.5 44.9 %slice-start = ((s8[6291456]{0:T(1024)(128)(4,1)}), s8[4194304]{0:T(1024)(128)(4,1)S(1)}, s32[]{:S(2)}) async-start(s8[6291456]{0:T(1024)(128)(4,1)} %bitcast.3), calls=%async_computation | async-start | bytes 8388608
  5.7 2.9 %copy-start = (bf16[768,4096]{1,0:T(8,128)(2,1)S(1)}, bf16[768,4096]{1,0:T(8,128)(2,1)}, u32[]{:S(2)}) copy-start(bf16[768,4096]{1,0:T(8,128)(2,1)} %k_ref.5) | copy-start | bytes 18874372
  8.6 2.8 %copy-start.1 = (bf16[768,4096]{1,0:T(8,128)(2,1)S(1)}, bf16[768,4096]{1,0:T(8,128)(2,1)}, u32[]{:S(2)}) copy-start(bf16[768,4096]{1,0:T(8,128)(2,1)} %v_ref.5) | copy-start | bytes 18874372
  11.4 38.4 %copy-start.4 = (s32[768]{0:T(1024)S(1)}, s32[768]{0:T(1024)}, u32[]{:S(2)}) copy-start(s32[768]{0:T(1024)} %param.11) | copy-start | bytes 9220
  11.4 39.0 %slice-start.1 = ((s8[6291456]{0:T(1024)(128)(4,1)}), s8[2097152]{0:T(1024)(128)(4,1)S(1)}, s32[]{:S(2)}) async-start(s8[6291456]{0:T(1024)(128)(4,1)} %bitcast.3), calls=%async_computation.1 | async-start | bytes 4194304
  11.4 39.0 %copy-start.3 = (f32[4096]{0:T(1024)S(1)}, f32[4096]{0:T(1024)}, u32[]{:S(2)}) copy-start(f32[4096]{0:T(1024)} %param.10) | copy-start | bytes 49156
  78.7 74.3 %slice-start.2 = ((s8[6291456]{0:T(1024)(128)(4,1)}), s8[4194304]{0:T(1024)(128)(4,1)S(1)}, s32[]{:S(2)}) async-start(s8[6291456]{0:T(1024)(128)(4,1)} %bitcast.5), calls=%async_computation.2 | async-start | bytes 8388608
  78.8 74.1 %slice-start.3 = ((s8[6291456]{0:T(1024)(128)(4,1)}), s8[2097152]{0:T(1024)(128)(4,1)S(1)}, s32[]{:S(2)}) async-start(s8[6291456]{0:T(1024)(128)(4,1)} %bitcast.5), calls=%async_computation.3 | async-start | bytes 4194304
  96.9 2.7 %copy-start.2 = (bf16[768,4096]{1,0:T(8,128)(2,1)}, bf16[768,4096]{1,0:T(8,128)(2,1)S(1)}, u32[]{:S(2)}) copy-start(bf16[768,4096]{1,0:T(8,128)(2,1)S(1)} %get-tuple-element.17.d_ref) | copy-start | bytes 18874372

commit v2 on v1

--- a/solution.py
+++ b/solution.py
@@ -29,14 +29,8 @@
     return lax.dot_general(a, b, (((0,), (0,)), ((), ())), preferred_element_type=F32)
 
 
-def state_kernel(k_ref, v_ref, last_ref, state_ref):
-    for h in range(k_ref.shape[1] // HD):
-        cols = slice(h * HD, (h + 1) * HD)
-        state_ref[cols, :] = dot_tn(k_ref[:, cols] * last_ref[...], v_ref[:, cols]).astype(BF16)
-
-
-def exchange_kernel(groups, reverse, state_ref, tag_ref, out_ref, got, tags, chain_in, chain_out,
-                    chain_tag, sends, back, sem_a, sem_b, sem_c, sem_d, sem_e):
+def exchange(groups, reverse, make_part, work, early, spread, pairs, state_ref, tag_ref, out_ref, got, tags,
+             chain_in, chain_out, chain_tag, sends, back, sem_a, sem_b, sem_c, sem_d, sem_e):
     me = lax.axis_index("ctx")
     group, member = me // MEMBERS, me % MEMBERS
     step = -1 if reverse else 1
@@ -84,11 +78,20 @@
         @pl.when(m != member)
         def _(m=m):
             label(m, member).start()
+
+        @pl.when(m == member)
+        def _(m=m):
+            tags[m] = tag_ref[...]
+
+    for m in range(MEMBERS):
+        make_part(m)
+
+        @pl.when(m != member)
+        def _(m=m):
             scatter(m, member).start()
 
         @pl.when(m == member)
         def _(m=m):
-            tags[m] = tag_ref[...]
             got[m] = state_ref[m * part:(m + 1) * part, :]
 
     @pl.when(place == 0)
@@ -105,10 +108,14 @@
     def _():
         chain_label().start()
 
+    work(0, early)
     for m in range(MEMBERS):
         @pl.when(m != member)
         def _(m=m):
             scatter(m, m).wait_recv()
+
+    middle = jnp.minimum(early + place * spread, pairs)
+    work(early, middle)
 
     @pl.when(place > 0)
     def _():
@@ -155,6 +162,7 @@
             def _(m=m, c=c, own=own):
                 back[m, c] = own
 
+    work(middle, pairs)
     for m in range(MEMBERS):
         for c in range(CHUNKS):
             @pl.when(m != member)
@@ -177,56 +185,95 @@
             chain(c).wait_send()
 
 
-def exchange(state, tag, blocks, reverse):
-    groups = blocks // MEMBERS
-    part = state.shape[0] // MEMBERS
+def exchange_scratch(width):
+    part = width // MEMBERS
     piece = part // CHUNKS
-    vmem = pl.BlockSpec(memory_space=pltpu.VMEM)
-    return pl.pallas_call(
-        functools.partial(exchange_kernel, groups, reverse),
-        out_shape=jax.ShapeDtypeStruct(state.shape, BF16),
-        in_specs=[vmem, vmem],
-        out_specs=vmem,
-        scratch_shapes=[
-            pltpu.VMEM((MEMBERS, part, HD), BF16),
-            pltpu.VMEM((MEMBERS, 8, HD), F32),
-            pltpu.VMEM((CHUNKS, piece, HD), BF16),
-            pltpu.VMEM((CHUNKS, piece, HD), BF16),
-            pltpu.VMEM((8, HD), F32),
-            pltpu.VMEM((MEMBERS, CHUNKS, piece, HD), BF16),
-            pltpu.VMEM((MEMBERS, CHUNKS, piece, HD), BF16),
-            pltpu.SemaphoreType.DMA((2, MEMBERS)),
-            pltpu.SemaphoreType.DMA((2, MEMBERS)),
-            pltpu.SemaphoreType.DMA((2, CHUNKS)),
-            pltpu.SemaphoreType.DMA((2,)),
-            pltpu.SemaphoreType.DMA((2, MEMBERS, CHUNKS)),
-        ],
-        compiler_params=pltpu.CompilerParams(collective_id=1 if reverse else 0, has_side_effects=True,
-                                             vmem_limit_bytes=16 * 2**20),
-        name="exchange_back" if reverse else "exchange_on",
-    )(state, tag)
-
-
-def forward_kernel(q_ref, k_ref, v_ref, og_ref, gain_ref, inc_ref, mask_ref, first_ref,
-                   att_ref, square_ref, cross_ref):
-    @pl.when(pl.program_id(0) == 0)
-    def _():
-        square_ref[...] = jnp.zeros_like(square_ref)
-        cross_ref[...] = jnp.zeros_like(cross_ref)
-
-    tokens = q_ref.shape[0]
-    for h in range(q_ref.shape[1] // HD):
-        cols = slice(h * HD, (h + 1) * HD)
-        for start in range(0, tokens, ROWS):
-            stop = start + ROWS
-            rows = slice(start, stop)
-            q = q_ref[rows, cols]
-            scores = dot_nt(q, k_ref[:stop, cols]).astype(BF16) * mask_ref[rows, :stop]
-            att = dot_nn(scores, v_ref[:stop, cols])
-            att += dot_nn(q * first_ref[rows, :], inc_ref[cols, :])
-            att_ref[rows, cols] = att
-            square_ref[rows, :] += att * att
-            cross_ref[rows, :] += gain_ref[:, cols] * og_ref[rows, cols].astype(F32) * att
+    return [
+        pltpu.VMEM((MEMBERS, part, HD), BF16),
+        pltpu.VMEM((MEMBERS, 8, HD), F32),
+        pltpu.VMEM((CHUNKS, piece, HD), BF16),
+        pltpu.VMEM((CHUNKS, piece, HD), BF16),
+        pltpu.VMEM((8, HD), F32),
+        pltpu.VMEM((MEMBERS, CHUNKS, piece, HD), BF16),
+        pltpu.VMEM((MEMBERS, CHUNKS, piece, HD), BF16),
+        pltpu.SemaphoreType.DMA((2, MEMBERS)),
+        pltpu.SemaphoreType.DMA((2, MEMBERS)),
+        pltpu.SemaphoreType.DMA((2, CHUNKS)),
+        pltpu.SemaphoreType.DMA((2,)),
+        pltpu.SemaphoreType.DMA((2, MEMBERS, CHUNKS)),
+    ]
+
+
+def head_cols(h):
+    return pl.ds(pl.multiple_of(h * HD, HD), HD)
+
+
+def forward_kernel(groups, q_hbm, k_hbm, v_hbm, og_hbm, gain_ref, tag_ref, mask_ref, first_ref, last_ref,
+                   att_hbm, inc_ref, square_ref, cross_ref, q_ref, k_ref, v_ref, og_ref, att_ref, state_ref,
+                   load_sem, store_sem, *scratch):
+    tokens, width = q_ref.shape
+    part = width // MEMBERS
+    pairs = width // HD // 2
+
+    def load(a, m):
+        source, target = ((k_hbm, k_ref), (v_hbm, v_ref), (q_hbm, q_ref), (og_hbm, og_ref))[a]
+        cols = pl.ds(m * part, part)
+        return pltpu.make_async_copy(source.at[:, cols], target.at[:, cols], load_sem.at[a, m])
+
+    def store(m):
+        cols = pl.ds(m * part, part)
+        return pltpu.make_async_copy(att_ref.at[:, cols], att_hbm.at[:, cols], store_sem.at[m])
+
+    for m in range(MEMBERS):
+        load(0, m).start()
+        load(1, m).start()
+    for a in (2, 3):
+        for m in range(MEMBERS):
+            load(a, m).start()
+
+    def make_part(m):
+        load(0, m).wait()
+        load(1, m).wait()
+        for h in range(m * part // HD, (m + 1) * part // HD):
+            cols = slice(h * HD, (h + 1) * HD)
+            state_ref[cols, :] = dot_tn(k_ref[:, cols] * last_ref[...], v_ref[:, cols]).astype(BF16)
+        if m == MEMBERS - 1:
+            for i in range(MEMBERS):
+                load(2, i).wait()
+
+    def work(low, high):
+        def pair(i, carry):
+            for h in (2 * i, 2 * i + 1):
+                cols = head_cols(h)
+                for start in range(0, tokens, ROWS):
+                    stop = start + ROWS
+                    rows = slice(start, stop)
+                    scores = dot_nt(q_ref[rows, cols], k_ref[:stop, cols]).astype(BF16) * mask_ref[rows, :stop]
+                    att_ref[rows, cols] = dot_nn(scores, v_ref[:stop, cols])
+            return carry
+        lax.fori_loop(low, high, pair, 0)
+
+    exchange(groups, False, make_part, work, pairs * 3 // 8, pairs // 4, pairs, state_ref, tag_ref, inc_ref, *scratch)
+
+    square_ref[...] = jnp.zeros_like(square_ref)
+    cross_ref[...] = jnp.zeros_like(cross_ref)
+    for m in range(MEMBERS):
+        load(3, m).wait()
+
+        def add(h, carry):
+            cols = head_cols(h)
+            inc = inc_ref[pl.ds(pl.multiple_of(h * HD, HD), HD), :]
+            for start in range(0, tokens, ROWS):
+                rows = slice(start, start + ROWS)
+                att = att_ref[rows, cols] + dot_nn(q_ref[rows, cols] * first_ref[rows, :], inc)
+                att_ref[rows, cols] = att
+                square_ref[rows, :] += att * att
+                cross_ref[rows, :] += gain_ref[:, cols] * og_ref[rows, cols].astype(F32) * att
+            return carry
+        lax.fori_loop(m * part // HD, (m + 1) * part // HD, add, 0)
+        store(m).start()
+    for m in range(MEMBERS):
+        store(m).wait()
 
 
 def delta_kernel(att_ref, og_ref, q_ref, gain_ref, inverse_ref, weight_ref, first_ref,
@@ -242,29 +289,79 @@
         state_ref[cols, :] = dot_tn(q_ref[:, cols] * first_ref[...], delta).astype(BF16)
 
 
-def backward_kernel(q_ref, k_ref, v_ref, d_ref, inc_ref, out_ref, mask_ref, first_ref, last_ref,
-                    gq_ref, gk_ref, gv_ref):
-    tokens = q_ref.shape[0]
-    for h in range(q_ref.shape[1] // HD):
-        cols = slice(h * HD, (h + 1) * HD)
-        grad_query = dot_nt(d_ref[:, cols] * first_ref[...], inc_ref[cols, :])
+def backward_kernel(groups, q_hbm, k_hbm, v_hbm, d_hbm, state_ref, tag_ref, inc_ref, mask_ref, first_ref,
+                    gq_hbm, gk_hbm, gv_hbm, out_ref, q_ref, k_ref, v_ref, d_ref,
+                    load_sem, store_sem, *scratch):
+    tokens, width = q_ref.shape
+    part = width // MEMBERS
+    pairs = width // HD // 2
+
+    def load(a, m):
+        source, target = ((q_hbm, q_ref), (k_hbm, k_ref), (v_hbm, v_ref), (d_hbm, d_ref))[a]
+        cols = pl.ds(m * part, part)
+        return pltpu.make_async_copy(source.at[:, cols], target.at[:, cols], load_sem.at[a, m])
+
+    def store(a):
+        source, target = ((q_ref, gq_hbm), (k_ref, gk_hbm), (v_ref, gv_hbm))[a]
+        return pltpu.make_async_copy(source, target, store_sem.at[a])
+
+    for m in range(MEMBERS):
+        for a in range(4):
+            load(a, m).start()
+
+    def make_part(m):
+        if m == MEMBERS - 1:
+            for a in range(4):
+                load(a, 0).wait()
+
+    def one(h):
+        cols = head_cols(h)
+        inc = inc_ref[pl.ds(pl.multiple_of(h * HD, HD), HD), :]
+        grad_query = dot_nt(d_ref[:, cols] * first_ref[...], inc)
         pieces = [grad_query[r:r + ROWS] for r in range(0, tokens, ROWS)]
         for start in range(0, tokens, ROWS):
             rows = slice(start, start + ROWS)
             k, v = k_ref[rows, cols], v_ref[rows, cols]
             q, d = q_ref[start:, cols], d_ref[start:, cols]
             mask = mask_ref[rows, start:]
-            last = last_ref[rows, :]
             scores = dot_nt(k, q).astype(BF16) * mask
             dscores = dot_nt(v, d).astype(BF16) * mask
-            gv_ref[rows, cols] = (dot_nn(scores, d) + dot_nn(k * last, out_ref[cols, :])).astype(BF16)
-            gk_ref[rows, cols] = (dot_nn(dscores, q) + dot_nt(v * last, out_ref[cols, :])).astype(BF16)
+            v_ref[rows, cols] = dot_nn(scores, d).astype(BF16)
+            k_ref[rows, cols] = dot_nn(dscores, q).astype(BF16)
             more = dot_tn(dscores, k)
             for i in range(start // ROWS, tokens // ROWS):
                 at = i * ROWS - start
                 pieces[i] = pieces[i] + more[at:at + ROWS]
         for i, piece in enumerate(pieces):
-            gq_ref[i * ROWS:(i + 1) * ROWS, cols] = piece.astype(BF16)
+            q_ref[i * ROWS:(i + 1) * ROWS, cols] = piece.astype(BF16)
+
+    def work(low, high):
+        def pair(i, carry):
+            one(2 * i)
+            one(2 * i + 1)
+            return carry
+        lax.fori_loop(low, high, pair, 0)
+        if isinstance(low, int) and low == 0:
+            for m in range(1, MEMBERS):
+                for a in range(4):
+                    load(a, m).wait()
+        if isinstance(high, int) and high == pairs:
+            for a in range(3):
+                store(a).start()
+
+    exchange(groups, True, make_part, work, pairs // MEMBERS, max(1, pairs // 8), pairs,
+             state_ref, tag_ref, out_ref, *scratch)
+    for a in range(3):
+        store(a).wait()
+
+
+def finish_kernel(k_ref, v_ref, gk_ref, gv_ref, out_ref, last_ref, grad_key_ref, grad_value_ref):
+    for h in range(k_ref.shape[1] // HD):
+        cols = slice(h * HD, (h + 1) * HD)
+        last = last_ref[...]
+        out = out_ref[cols, :]
+        grad_key_ref[:, cols] = (gk_ref[:, cols].astype(F32) + dot_nt(v_ref[:, cols] * last, out)).astype(BF16)
+        grad_value_ref[:, cols] = (gv_ref[:, cols].astype(F32) + dot_nn(k_ref[:, cols] * last, out)).astype(BF16)
 
 
 def shards(blocks, queries, keys, values, out_grad, gain, doc_ids):
@@ -285,28 +382,31 @@
     each = 2
     wide = each * HD
     grid = (heads // each,)
-    head_cols = pl.BlockSpec((tokens, wide), lambda i: (0, i))
+    cols_spec = pl.BlockSpec((tokens, wide), lambda i: (0, i))
     gain_cols = pl.BlockSpec((1, wide), lambda i: (0, i))
     head_state = pl.BlockSpec((wide, HD), lambda i: (i, 0))
     whole = pl.BlockSpec((tokens, HD), lambda i: (0, 0))
-    whole_mask = pl.BlockSpec((tokens, tokens), lambda i: (0, 0))
     state_shape = jax.ShapeDtypeStruct((width, HD), BF16)
     flat_shape = jax.ShapeDtypeStruct((tokens, width), BF16)
     sums_shape = jax.ShapeDtypeStruct((tokens, HD), F32)
     params = pltpu.CompilerParams(vmem_limit_bytes=40 * 2**20)
 
-    own_state = pl.pallas_call(
-        state_kernel, grid=grid, in_specs=[head_cols, head_cols, whole], out_specs=head_state,
-        out_shape=state_shape, compiler_params=params, name="block_state",
-    )(keys, values, last_rows)
-    incoming = exchange(own_state, tag, blocks, False)
-    attended, squares, crosses = pl.pallas_call(
-        forward_kernel, grid=grid,
-        in_specs=[head_cols, head_cols, head_cols, head_cols, gain_cols, head_state, whole_mask, whole],
-        out_specs=[head_cols, whole, whole],
-        out_shape=[jax.ShapeDtypeStruct((tokens, width), F32), sums_shape, sums_shape],
-        compiler_params=params, name="attend",
-    )(queries, keys, values, out_grad, gain, incoming, mask, first_rows)
+    groups = blocks // MEMBERS
+    vmem = pl.BlockSpec(memory_space=pltpu.VMEM)
+    hbm = pl.BlockSpec(memory_space=pl.ANY)
+    held = pltpu.VMEM((tokens, width), BF16)
+    att_shape = jax.ShapeDtypeStruct((tokens, width), F32)
+    attended, incoming, squares, crosses = pl.pallas_call(
+        functools.partial(forward_kernel, groups),
+        in_specs=[hbm] * 4 + [vmem] * 5,
+        out_specs=[hbm, vmem, vmem, vmem],
+        out_shape=[att_shape, state_shape, sums_shape, sums_shape],
+        scratch_shapes=[held, held, held, held, pltpu.VMEM((tokens, width), F32), pltpu.VMEM((width, HD), BF16),
+                        pltpu.SemaphoreType.DMA((4, MEMBERS)), pltpu.SemaphoreType.DMA((MEMBERS,))]
+        + exchange_scratch(width),
+        compiler_params=pltpu.CompilerParams(collective_id=0, has_side_effects=True, vmem_limit_bytes=58 * 2**20),
+        name="attend",
+    )(queries, keys, values, out_grad, gain, tag, mask, first_rows, last_rows)
     square_sum, cross_sum = lax.psum((jnp.sum(squares, axis=1), jnp.sum(crosses, axis=1)), "tp")
     inverse = lax.rsqrt(square_sum / width_all + NORM_EPS)
     weight = inverse**3 * cross_sum / width_all
@@ -314,18 +414,28 @@
     weight = jnp.broadcast_to(weight[:, None], (tokens, HD))
     normed, delta, own_reverse = pl.pallas_call(
         delta_kernel, grid=grid,
-        in_specs=[head_cols, head_cols, head_cols, gain_cols, whole, whole, whole],
-        out_specs=[head_cols, head_cols, head_state],
+        in_specs=[cols_spec, cols_spec, cols_spec, gain_cols, whole, whole, whole],
+        out_specs=[cols_spec, cols_spec, head_state],
         out_shape=[flat_shape, flat_shape, state_shape],
         compiler_params=params, name="delta",
     )(attended, out_grad, queries, gain, inverse, weight, first_rows)
-    outgoing = exchange(own_reverse, tag, blocks, True)
-    grad_query, grad_key, grad_value = pl.pallas_call(
-        backward_kernel, grid=grid,
-        in_specs=[head_cols] * 4 + [head_state] * 2 + [whole_mask, whole, whole],
-        out_specs=[head_cols] * 3, out_shape=[flat_shape] * 3,
-        compiler_params=params, name="grads",
-    )(queries, keys, values, delta, incoming, outgoing, mask_t, first_rows, last_rows)
+    grad_query, key_part, value_part, outgoing = pl.pallas_call(
+        functools.partial(backward_kernel, groups),
+        in_specs=[hbm] * 4 + [vmem] * 5,
+        out_specs=[hbm, hbm, hbm, vmem],
+        out_shape=[flat_shape, flat_shape, flat_shape, state_shape],
+        scratch_shapes=[held, held, held, held,
+                        pltpu.SemaphoreType.DMA((4, MEMBERS)), pltpu.SemaphoreType.DMA((3,))]
+        + exchange_scratch(width),
+        compiler_params=pltpu.CompilerParams(collective_id=1, has_side_effects=True, vmem_limit_bytes=58 * 2**20),
+        name="grads",
+    )(queries, keys, values, delta, own_reverse, tag, incoming, mask_t, first_rows)
+    grad_key, grad_value = pl.pallas_call(
+        finish_kernel, grid=grid,
+        in_specs=[cols_spec] * 4 + [head_state, whole],
+        out_specs=[cols_spec] * 2, out_shape=[flat_shape] * 2,
+        compiler_params=params, name="finish",
+    )(keys, values, key_part, value_part, outgoing, last_rows)
     return normed, grad_query, grad_key, grad_value
 
 

time: 200 us -> 194 us (0.970)
  Pallas kernels: 181 us -> 160 us
  local copies, waits for them, and re-layouts: 10.5 us -> 20.8 us
  other arithmetic: 4.19 us -> 8.34 us
    pallas_call x6 -> x4, Pallas kernels: 181 us -> 160 us  [the longest x1 79.1 us: shards(): pl.pallas_call(functools.partial(backward_kernel, groups), in_specs=[hbm]...]
    unnamed x18 -> x17, local copies, waits for them, and re-layouts: 8.4 us -> 16.8 us
    convert_element_type x1, other arithmetic: 0.55 us -> 2.71 us  [shards(): mask_t = (same & (position[:, None] <= position[None, :])).astype(BF16)]
where the time goes in v2:
time: 194 us; the launch traced here: 192 us
  Pallas kernels  160 us (82%)
  local copies, waits for them, and re-layouts  20.8 us (11%)
  other arithmetic  8.34 us (4%)
  blocking collectives  2.5 us (1%)
    pallas_call x1, Pallas kernels, shards(): pl.pallas_call(functools.partial(backward_kernel, groups), in_specs=[hbm]...  79.1 us
    pallas_call x1, Pallas kernels, shards(): pl.pallas_call(functools.partial(forward_kernel, groups), in_specs=[hbm]...  47.8 us
    pallas_call x1, Pallas kernels, shards(): pl.pallas_call(delta_kernel, grid=grid, in_specs=[cols_spec, cols_spec, c...  17.2 us
    unnamed x17, local copies, waits for them, and re-layouts  16.8 us
    pallas_call x1, Pallas kernels, shards(): pl.pallas_call(finish_kernel, grid=grid, in_specs=[cols_spec] * 4 + [head...  15.9 us

profile of v2, /device:TPU:0, one launch (start us, length us, event | category | flops | bytes accessed | tf_op | source)
XLA Modules:
  0.0 192.3 jit_solution(1471828946088623089)
XLA Ops:
  0.6 1.3 fusion.5
  2.0 1.3 fusion.4
  3.3 2.0 %compare_convert_fusion = (bf16[768]{0:T(1024)(128)(2,1)S(1)}, bf16[768]{0:T(1024)(128)(2,1)S(1)}) fusion(s32[768]{0:T(1024)} %param.11, s32[]{:T(128)} %bitcast.2, s32[]{:T(128)} %bitcast.1), kind=kLoop, calls=%fused_computation.10 | loop fusion | flops 3072 | bytes 6152 | tf_op jit(solution)/shard_map/convert_element_type | solution.py:377
  5.3 0.7 broadcast_in_dim.23.tag_ref
  5.9 0.8 broadcast_in_dim.25.last_ref
  6.8 0.8 broadcast_in_dim.24.first_ref
  7.6 2.7 %fusion.1 = (bf16[768,768]{1,0:T(8,128)(2,1)}, bf16[768,768]{1,0:T(8,128)(2,1)}) fusion(s32[768]{0:T(1024)} %param.11), kind=kLoop, calls=%fused_computation.5 | loop fusion | flops 4128768 | bytes 2362368 | tf_op jit(solution)/shard_map/convert_element_type | solution.py:374
  10.3 0.0 copy-start.3
  10.3 0.0 copy-start.7
  10.3 47.8 %attend.1 = (f32[768,4096]{1,0:T(8,128)}, bf16[4096,128]{1,0:T(8,128)(2,1)}, f32[768,128]{1,0:T(8,128)}, f32[768,128]{1,0:T(8,128)}) custom-call(bf16[768,4096]{1,0:T(8,128)(2,1)} %q_hbm.3, bf16[768,4096]{1,0:T(8,128)(2,1)} %k_ref.1, bf16[768,4096]{1,0:T(8,128)(2,1)} %v_ref.1, bf16[768,4096]{1,0:T(8,128)(2,1)} %og_ref.1, f32[1,4096]{1,0:T(1,128)} %bitcast.3, ...), custom_call_target="tpu_custom_call" | custom-call | tf_op jit(solution)/shard_map/attend/pallas_call | solution.py:399
  58.1 1.2 reduce_sum.18
  59.3 1.2 reduce_sum.19
  60.5 2.5 %all-reduce = (f32[768]{0:T(1024)S(1)}, f32[768]{0:T(1024)S(1)}) all-reduce(f32[768]{0:T(1024)S(1)} %reduce_sum.18, f32[768]{0:T(1024)S(1)} %reduce_sum.19), channel_id=1, replica_groups=mesh['ctx'=16,'tp'=2] {'tp'}, use_global_device_ids=true, to_apply=%region_1.2 | all-reduce | flops 1536 | bytes 12288 | tf_op jit(solution)/shard_map/psum | solution.py:410
  63.0 0.2 broadcast_in_dim.27.weight_ref
  63.2 0.2 broadcast_in_dim.26.inverse_ref
  63.3 0.0 copy-done.3
  63.4 0.0 copy-done.7
  63.4 17.2 %delta.1 = (bf16[768,4096]{1,0:T(8,128)(2,1)}, bf16[768,4096]{1,0:T(8,128)(2,1)S(1)}, bf16[4096,128]{1,0:T(8,128)(2,1)S(1)}) custom-call(f32[768,4096]{1,0:T(8,128)} %get-tuple-element.17.att_ref, bf16[768,4096]{1,0:T(8,128)(2,1)} %og_ref.1, bf16[768,4096]{1,0:T(8,128)(2,1)} %q_hbm.3, f32[1,4096]{1,0:T(1,128)S(1)} %bitcast.4, ...), custom_call_target="tpu_custom_call" | custom-call | tf_op jit(solution)/shard_map/delta/pallas_call | solution.py:415
  80.5 0.0 copy-start.2
  80.6 2.7 %copy-done.2 = bf16[768,4096]{1,0:T(8,128)(2,1)} copy-done((bf16[768,4096]{1,0:T(8,128)(2,1)}, bf16[768,4096]{1,0:T(8,128)(2,1)S(1)}, u32[]{:S(2)}) %copy-start.2) | copy-done | bytes 6291480
  83.3 0.0 copy-start.6
  83.3 1.0 copy-done.6
  84.2 0.0 copy-start.4
  84.2 79.1 %grads.1 = (bf16[768,4096]{1,0:T(8,128)(2,1)}, bf16[768,4096]{1,0:T(8,128)(2,1)}, bf16[768,4096]{1,0:T(8,128)(2,1)}, bf16[4096,128]{1,0:T(8,128)(2,1)}) custom-call(bf16[768,4096]{1,0:T(8,128)(2,1)} %q_hbm.3, bf16[768,4096]{1,0:T(8,128)(2,1)} %k_ref.1, bf16[768,4096]{1,0:T(8,128)(2,1)} %v_ref.1, bf16[768,4096]{1,0:T(8,128)(2,1)} %copy-done.2, ...), custom_call_target="tpu_custom_call" | custom-call | tf_op jit(solution)/shard_map/grads/pallas_call | solution.py:422
  163.3 0.0 copy-done.4
  163.3 0.0 copy-start
  163.3 2.8 %copy-done = bf16[768,4096]{1,0:T(8,128)(2,1)S(1)} copy-done((bf16[768,4096]{1,0:T(8,128)(2,1)S(1)}, bf16[768,4096]{1,0:T(8,128)(2,1)}, u32[]{:S(2)}) %copy-start) | copy-done | bytes 6291480
  166.1 0.0 copy-start.1
  166.1 2.8 %copy-done.1 = bf16[768,4096]{1,0:T(8,128)(2,1)S(1)} copy-done((bf16[768,4096]{1,0:T(8,128)(2,1)S(1)}, bf16[768,4096]{1,0:T(8,128)(2,1)}, u32[]{:S(2)}) %copy-start.1) | copy-done | bytes 6291480
  168.9 0.0 copy-start.5
  168.9 1.2 copy-done.5
  170.1 15.9 %finish.1 = (bf16[768,4096]{1,0:T(8,128)(2,1)}, bf16[768,4096]{1,0:T(8,128)(2,1)}) custom-call(bf16[768,4096]{1,0:T(8,128)(2,1)S(1)} %copy-done, bf16[768,4096]{1,0:T(8,128)(2,1)S(1)} %copy-done.1, bf16[768,4096]{1,0:T(8,128)(2,1)} %get-tuple-element.25.gk_ref, bf16[768,4096]{1,0:T(8,128)(2,1)} %get-tuple-element.26.gv_ref, bf16[4096,128]{1,0:T(8,128)(2,1)S(1)} %copy-done.5, ...), custom_call_target="tpu_custom_call" | custom-call | tf_op jit(solution)/shard_map/finish/pallas_call | solution.py:433
  186.0 6.3 %copy.11 = bf16[768,4096]{1,0:T(8,128)(2,1)} copy(bf16[768,4096]{1,0:T(8,128)(2,1)} %get-tuple-element.45) | data formatting | bytes 12582912
  (1 shorter events, 0.0 us)
Async XLA Ops:
  10.3 53.0 %copy-start.3 = (bf16[768,128]{1,0:T(8,128)(2,1)S(1)}, bf16[768,128]{1,0:T(8,128)(2,1)}, u32[]{:S(2)}) copy-start(bf16[768,128]{1,0:T(8,128)(2,1)} %broadcast_in_dim.24.first_ref) | copy-start | bytes 589828
  10.3 53.0 %copy-start.7 = (f32[4096]{0:T(1024)S(1)}, f32[4096]{0:T(1024)}, u32[]{:S(2)}) copy-start(f32[4096]{0:T(1024)} %param.10) | copy-start | bytes 49156
  80.5 2.7 %copy-start.2 = (bf16[768,4096]{1,0:T(8,128)(2,1)}, bf16[768,4096]{1,0:T(8,128)(2,1)S(1)}, u32[]{:S(2)}) copy-start(bf16[768,4096]{1,0:T(8,128)(2,1)S(1)} %get-tuple-element.21.d_hbm) | copy-start | bytes 18874372
  83.3 1.0 copy-start.6
  84.2 79.1 %copy-start.4 = (bf16[768,128]{1,0:T(8,128)(2,1)S(1)}, bf16[768,128]{1,0:T(8,128)(2,1)}, u32[]{:S(2)}) copy-start(bf16[768,128]{1,0:T(8,128)(2,1)} %broadcast_in_dim.25.last_ref) | copy-start | bytes 589828
  163.3 2.8 %copy-start = (bf16[768,4096]{1,0:T(8,128)(2,1)S(1)}, bf16[768,4096]{1,0:T(8,128)(2,1)}, u32[]{:S(2)}) copy-start(bf16[768,4096]{1,0:T(8,128)(2,1)} %k_ref.1) | copy-start | bytes 18874372
  166.1 2.8 %copy-start.1 = (bf16[768,4096]{1,0:T(8,128)(2,1)S(1)}, bf16[768,4096]{1,0:T(8,128)(2,1)}, u32[]{:S(2)}) copy-start(bf16[768,4096]{1,0:T(8,128)(2,1)} %v_ref.1) | copy-start | bytes 18874372
  168.9 1.2 copy-start.5
